TPU v7x, 32 devices: a whole 2x2x4 slice. The times are simulated.
32 devices in a mesh: poles: 2 (over y), grid: 16 (over z, x, core).
Axes of the slice: x: 2, y: 2, z: 4, core: 2. Of those that a mesh axis runs over, the one named last changes fastest.
Arguments:
- inverse_block: float32 [2, 2, 1024, 1024], P('poles', None, 'grid'), as said below
- factor_block: float32 [2, 2, 1024, 512], P('poles', None, 'grid'), may hold values from -6 to 6
- diag_inverse: float32 [2, 2, 512, 512], P('poles', None, 'grid'), may hold values from -6 to 6
- residues: float32 [2, 2], P('poles'), may hold values from -4 to 4
- block_owner: int32 [16], replicated, may hold values from 0 to 15, as said below
- row_count: int32 [16], replicated, may hold values from 1 to 64, 768 in all
Outputs:
- density_off: float32 [2, 1024, 512], P(None, 'grid')
- density_diag: float32 [2, 512, 512], P(None, 'grid')
Inputs may be any that keep to these rules, and one draw needn't show every extreme that they name: block_owner is a permutation: natural ancestor row block b (natural rows b * 64 to b * 64 + 63) sits at block position block_owner[b] of the arrays split over grid. With its rows put back in natural order, each pole's inverse_block (real part and imaginary part each) is a symmetric matrix.
All inputs are finite; a program needn't handle non-finite values.
Results may differ from a plain program's by a relative error of at most 0.00007.
Values sent between devices are 32-bit elements; how exact they have to be, the bound alone decides.
A program may use at most 128 MiB of HBM per device.

v0:
```python
import jax
import jax.numpy as jnp
from jax import lax
from jax.sharding import PartitionSpec as P

HIGHEST_PRECISION = lax.Precision.HIGHEST


def product(left, right):
    return jnp.dot(left, right, preferred_element_type=jnp.float32, precision=HIGHEST_PRECISION)


def complex_product(left_real, left_imag, right_real, right_imag):
    return (
        product(left_real, right_real) - product(left_imag, right_imag),
        product(left_real, right_imag) + product(left_imag, right_real),
    )


def weigh(weights, values):
    return jnp.stack(
        [
            weights[0] * values[0] - weights[1] * values[1],
            weights[0] * values[1] + weights[1] * values[0],
        ]
    )


def natural_columns(inverse_of, amount, own_rows):
    stored = jnp.arange(amount, dtype=jnp.int32)
    return inverse_of[stored // own_rows] * own_rows + stored % own_rows


def per_device(inverse_block, factor_block, diag_inverse, residues, block_owner, row_count):
    inverse_rows = inverse_block[0]
    factor_rows = factor_block[0]
    diag_rows = diag_inverse[0]
    weights = residues[0]
    own_rows = factor_rows.shape[1]
    nblocks = block_owner.shape[0]
    blocks = jnp.arange(nblocks, dtype=jnp.int32)
    inverse_of = jnp.zeros((nblocks,), jnp.int32).at[block_owner].set(blocks)
    position = lax.axis_index("grid")
    own_block = jnp.sum(jnp.where(block_owner == position, blocks, 0))
    live_count = jnp.sum(jnp.where(blocks == own_block, row_count, 0))
    live_rows = (jnp.arange(own_rows, dtype=jnp.int32) < live_count).astype(jnp.float32)
    masked = factor_rows * live_rows[None, :, None]
    shard_piece = lax.all_gather(masked, "grid", axis=1, tiled=True)
    columns = jnp.take(
        inverse_rows, natural_columns(inverse_of, shard_piece.shape[1], own_rows), axis=2
    )
    real_part, imag_part = complex_product(columns[0], columns[1], shard_piece[0], shard_piece[1])
    offdiag = -jnp.stack([real_part, imag_part])
    offdiag = offdiag * live_rows[None, :, None]
    gram_real, gram_imag = complex_product(masked[0].T, masked[1].T, offdiag[0], offdiag[1])
    gram = jnp.stack([gram_real, gram_imag])
    row_share = lax.psum_scatter(gram, "grid", scatter_dimension=1, tiled=True)
    diag_term = weigh(weights, diag_rows - row_share)
    density_off, density_diag = lax.psum((weigh(weights, offdiag), diag_term), "poles")
    return (density_off, density_diag)


def solution(mesh):
    placed = (
        P("poles", None, "grid", None),
        P("poles", None, "grid", None),
        P("poles", None, "grid", None),
        P("poles", None),
        P(),
        P(),
    )
    return jax.shard_map(
        per_device,
        mesh=mesh,
        in_specs=placed,
        out_specs=(P(None, "grid", None), P(None, "grid", None)),
        check_vma=False,
    )
```

profile of v0, /device:TPU:0, one launch (start us, length us, event | category | flops | bytes accessed | tf_op | source)
XLA Modules:
  0.0 178.8 jit_solution(6187713833646166043)
XLA Ops:
  7.2 0.0 all-gather.2.cloned.1.call-start
  7.2 1.3 fusion.26
  8.5 1.9 %fusion.27 = s32[]{:T(128)} fusion(s32[16]{0:T(128)} %param.11, s32[]{:T(128)} %get-tuple-element.14), kind=kLoop, calls=%fused_computation.78 | loop fusion | flops 47 | bytes 72 | tf_op jit(solution)/shard_map/reduce_sum | solution.py:45
  10.4 0.6 compare_convert_fusion
  11.1 1.7 bitcast_multiply_fusion
  12.8 0.0 all-gather.2.cloned.1.call-update
  12.9 0.0 reduce-scatter.2.cloned.1.call-start
  12.9 1.5 copy.8
  14.4 0.6 scatter_custom_fusion
  15.3 0.7 fusion.32
  16.0 4.3 %compare_select_fusion.2 = s32[1024,1]{0,1:T(1,128)S(1)} fusion(s32[]{:T(128)} %bitcast.10, s32[]{:T(128)} %bitcast.11, s32[]{:T(128)} %bitcast.12, s32[]{:T(128)} %bitcast.13, s32[]{:T(128)} %bitcast.14, s32[]{:T(128)} %bitcast.16, s32[]{:T(128)} %bitcast.15), kind=kLoop, calls=%fused_computation.51 | loop fusion | flops 23552 | bytes 4124 | tf_op jit(solution)/shard_map/gather | solution.py:31
  20.4 5.7 %compare_and_fusion = (pred[1024]{0:T(1024)(128)(4,1)S(1)}, s32[1024]{0:T(1024)S(1)}) fusion(pred[1024]{0:T(1024)(128)(4,1)S(1)} %compare_reduce_fusion, pred[1024]{0:T(1024)(128)(4,1)S(1)} %compare_reduce_fusion.1, pred[1024]{0:T(1024)(128)(4,1)S(1)} %compare_reduce_fusion.2, pred[1024]{0:T(1024)(128)(4,1)S(1)} %compare_reduce_fusion.3, ...), kind=kLoop, calls=%fused_computation.71 | loop fusion | flops 23552 | bytes 18468 | tf_op jit(solution)/shard_map/jit(_take)/and | solution.py:49
  26.1 3.5 %gather_fusion = f32[1024,2,64]{2,1,0:T(2,128)S(1)} fusion(f32[2,64,1024]{1,0,2:T(2,128)S(1)} %bitcast.80, s32[1024]{0:T(1024)S(1)} %broadcast_clamp_fusion), kind=kCustom, calls=%fused_computation | custom fusion | bytes 1052672 | tf_op jit(solution)/shard_map/jit(_take)/gather | solution.py:49
  29.6 3.7 %select_bitcast_fusion = f32[2,64,1024]{1,0,2:T(2,128)S(1)} fusion(f32[1024,2,64]{2,1,0:T(2,128)S(1)} %gather_fusion, pred[1024]{0:T(1024)(128)(4,1)S(1)} %get-tuple-element.4), kind=kLoop, calls=%fused_computation.17 | loop fusion | flops 131072 | bytes 1049600 | tf_op jit(solution)/shard_map/jit(_take)/select_n | solution.py:49
  33.4 0.8 fusion.30
  34.2 32.3 %all-gather.2.cloned.1.call-done = f32[2,1024,512]{2,1,0:T(8,128)} async-done(((f32[2,64,512]{2,1,0:T(8,128)}), f32[2,1024,512]{2,1,0:T(8,128)}) %all-gather.2.cloned.1.call-update) | async-done | bytes 4194320 | tf_op jit(solution)/shard_map/all_gather | solution.py:48
  66.5 0.0 copy-start
  66.5 3.0 %fusion.1 = f32[64,512]{1,0:T(8,128)S(1)} fusion(f32[64,1024]{0,1:T(8,128)S(1)} %bitcast.76, f32[2,1024,512]{2,1,0:T(8,128)} %all-gather.2.cloned.1.call-done), kind=kOutput, calls=%fused_computation.6 | convolution fusion | flops 402653184 | bytes 2490368 | tf_op jit(solution)/shard_map/dot_general | solution.py:10
  69.5 2.9 %fusion = f32[64,512]{1,0:T(8,128)S(1)} fusion(f32[64,1024]{0,1:T(8,128)S(1)} %bitcast.78, f32[2,1024,512]{2,1,0:T(8,128)} %all-gather.2.cloned.1.call-done), kind=kOutput, calls=%fused_computation.5 | convolution fusion | flops 402653184 | bytes 2490368 | tf_op jit(solution)/shard_map/dot_general | solution.py:10
  72.4 0.0 copy-done
  72.4 1.3 fusion.7
  73.6 0.0 copy-start.1
  73.7 1.3 fusion.9
  74.9 0.1 fusion.10
  75.0 0.0 copy-done.1
  75.0 1.0 fusion.15
  76.1 1.0 fusion.11
  77.1 1.0 fusion.5
  78.2 1.0 fusion.4
  79.2 1.5 pad_maximum_fusion
  80.7 0.0 copy-start.3
  80.7 0.0 copy-start.2
  80.7 0.0 reduce-scatter.2.cloned.1.call-update
  80.8 0.0 all-reduce.3.cloned.1.call-start
  80.8 0.6 copy-done.3
  81.4 0.6 fusion.31
  82.0 1.4 multiply_subtract_fusion
  83.4 0.7 pad_maximum_fusion.1
  84.1 56.8 %reduce-scatter.2.cloned.1.call-done = f32[2,32,512]{2,1,0:T(8,128)} async-done(((f32[2,512,512]{2,1,0:T(8,128)}), f32[2,32,512]{2,1,0:T(8,128)}) %reduce-scatter.2.cloned.1.call-update) | async-done | bytes 131088 | tf_op jit(solution)/shard_map/reduce_scatter | solution.py:57
  141.0 0.0 copy-done.2
  141.0 0.9 bitcast_subtract_fusion
  141.9 1.3 multiply_subtract_fusion.1
  143.2 0.7 pad_maximum_fusion.2
  143.9 0.0 all-reduce.3.cloned.1.call-update
  143.9 25.1 %all-reduce.3.cloned.1.call-done = (f32[2,64,512]{2,1,0:T(8,128)}, f32[2,32,512]{2,1,0:T(8,128)}) async-done(((f32[2,64,512]{2,1,0:T(8,128)}, f32[2,32,512]{2,1,0:T(8,128)}), (f32[2,64,512]{2,1,0:T(8,128)}, f32[2,32,512]{2,1,0:T(8,128)})) %all-reduce.3.cloned.1.call-update) | async-done | bytes 393232 | tf_op jit(solution)/shard_map/psum | solution.py:59
  169.0 1.7 copy.11
  170.7 1.6 copy.12
  (12 shorter events, 0.3 us)
Async XLA Ops:
  7.2 59.3 %all-gather.2.cloned.1.call-start = ((), (), s32[]{:S(2)}) async-start(), calls=%async_computation.1 | async-start | bytes 4456448 | tf_op jit(solution)/shard_map/all_gather | solution.py:48
  12.9 128.1 %reduce-scatter.2.cloned.1.call-start = ((), (), s32[]{:S(2)}) async-start(), calls=%async_computation.2 | async-start | bytes 2228224 | tf_op jit(solution)/shard_map/reduce_scatter | solution.py:57
  66.5 5.9 %copy-start = (f32[2,1024,512]{2,1,0:T(8,128)S(1)}, f32[2,1024,512]{2,1,0:T(8,128)}, u32[]{:S(2)}) copy-start(f32[2,1024,512]{2,1,0:T(8,128)} %all-gather.2.cloned.1.call-done) | copy-start | bytes 12582916
  73.6 1.4 copy-start.1
  80.7 0.7 copy-start.3
  80.7 60.2 %copy-start.2 = (f32[1,2,32,512]{3,2,1,0:T(8,128)S(1)}, f32[1,2,32,512]{3,2,1,0:T(8,128)}, u32[]{:S(2)}) copy-start(f32[1,2,32,512]{3,2,1,0:T(8,128)} %param.8) | copy-start | bytes 393220
  80.8 88.3 %all-reduce.3.cloned.1.call-start = ((), (), s32[]{:S(2)}) async-start(), calls=%async_computation.3 | async-start | bytes 786432 | tf_op jit(solution)/shard_map/psum | solution.py:59
Sparse Core Ops, SparseCore 0:
  13.0 53.4 all-gather.1
  80.9 60.0 reduce-scatter.1
  144.1 24.9 all-reduce.2
where the time goes:
time: 179 us
  waiting for transfers between devices  114 us (64%)
  other arithmetic  26.3 us (15%)
  between operations  13.9 us (8%)
  matrix products  12.6 us (7%)
  local copies, waits for them, and re-layouts  11.6 us (6%)
    reduce_scatter x1, waiting for transfers between devices, per_device(): row_share = lax.psum_scatter(gram, 'grid', scatter_dimension=1, tiled=True)  56.8 us
    all_gather x1, waiting for transfers between devices, per_device(): shard_piece = lax.all_gather(masked, 'grid', axis=1, tiled=True)  32.3 us
    psum x1, waiting for transfers between devices, per_device(): lax.psum((weigh(weights, offdiag), diag_term), 'poles')  25.1 us
    dot_general x8, matrix products, product(): jnp.dot(left, right, preferred_element_type=jnp.float32, precision=HIGHES...  12.6 us
    and x1, other arithmetic, per_device(): jnp.take(inverse_rows, natural_columns(inverse_of, shard_piece.shape[1],...  5.65 us
    unnamed x11, local copies, waits for them, and re-layouts  5.28 us
    gather x10, other arithmetic, natural_columns(): return inverse_of[stored // own_rows] * own_rows + stored % own_rows  4.65 us
    select_n x2, other arithmetic, per_device(): jnp.take(inverse_rows, natural_columns(inverse_of, shard_piece.shape[1],...  3.75 us
  transfers between devices with their start and end apart: 3, of which 3 were waited for; matrix products, arithmetic and copies ran while one was open for 13% of the time, Pallas kernels for 0%

commit v1 on v0

v1 whole, which is shorter than its diff:
```python
import functools

import jax
import jax.numpy as jnp
from jax import lax
from jax.experimental import pallas as pl
from jax.experimental.pallas import tpu as pltpu
from jax.sharding import PartitionSpec as P

BF16 = jnp.bfloat16
F32 = jnp.float32


def split(values):
    high = values.astype(BF16)
    return high, (values - high.astype(F32)).astype(BF16)


def dot(left, right):
    return jnp.dot(left, right, preferred_element_type=F32)


def pair_product(left4, right_real, right_imag, rows):
    width = right_real.shape[1]
    real_high, real_low = split(right_real)
    imag_high, imag_low = split(right_imag)
    first = dot(left4, jnp.concatenate([real_high, imag_high], axis=1))
    second = dot(left4[: 2 * rows], jnp.concatenate([real_low, imag_low], axis=1))
    by_real = first[: 2 * rows] + first[2 * rows :] + second
    rr, ri = by_real[:rows, :width], by_real[:rows, width:]
    ir, ii = by_real[rows:, :width], by_real[rows:, width:]
    return rr - ii, ri + ir


def nearest(place, step, amount):
    near = jnp.minimum(place, amount - 1 - place)
    half = (step + 1) // 2
    both = jnp.where(step % 2 == 1, place + half, place - half)
    far = jnp.where(place < amount - 1 - place, place + (step - near), place - (step - near))
    return jnp.where(step <= 2 * near, both, far)


def kernel(
    dims, a_ref, f_ref, d_ref, w_ref, owner_ref, count_ref, off_out, diag_out,
    full, a4, off_all, ft, gram, gram_in, pole_off, pole_diag,
    full_send, full_recv, off_send, off_recv, gram_send, gram_recv, po_send, po_recv, pd_send, pd_recv,
):
    poles, outer, inner = dims
    n = outer * inner * 2
    group = inner * 2
    rows, width = f_ref.shape[1], f_ref.shape[2]
    total_rows = a_ref.shape[2]
    share = d_ref.shape[1]
    me = lax.axis_index("grid")
    pole = lax.axis_index("poles")
    z, x, c = me // group, (me // 2) % inner, me % 2

    def index(at_z, at_x, at_c):
        return at_z * group + at_x * 2 + at_c

    barrier = pltpu.get_barrier_semaphore()

    def greet(target):
        pl.semaphore_signal(barrier, inc=1, device_id=target, device_id_type=pl.DeviceIdType.MESH)

    greet((pole, index(z, x, 1 - c)))
    for k in range(1, outer):
        greet((pole, index((z + k) % outer, x, c)))
    for k in range(1, poles):
        greet(((pole + k) % poles, me))
    pl.when(x > 0)(lambda: greet((pole, index(z, x - 1, c))))
    pl.when(x < inner - 1)(lambda: greet((pole, index(z, x + 1, c))))

    live_count = jnp.int32(0)
    for b in range(n):
        live_count = live_count + jnp.where(owner_ref[b] == me, count_ref[b], 0)
    live = (lax.broadcasted_iota(jnp.int32, (rows, width), 0) < live_count).astype(F32)
    full[me, 0] = f_ref[0] * live
    full[me, 1] = f_ref[1] * live

    beside = jnp.where(x > 0, 1, 0) + jnp.where(x < inner - 1, 1, 0)
    pl.semaphore_wait(barrier, outer + poles - 1 + beside)

    def full_copy(slot, way, target):
        return pltpu.make_async_remote_copy(
            src_ref=full.at[slot], dst_ref=full.at[slot],
            send_sem=full_send.at[slot, way], recv_sem=full_recv.at[slot],
            device_id=(pole, target), device_id_type=pl.DeviceIdType.MESH,
        )

    def each_full(from_z, from_x, act):
        slot = index(from_z, from_x, c)
        mine = from_x == x
        pl.when(mine & (z < outer - 1) & (from_z <= z))(lambda: act(full_copy(slot, 0, index(z + 1, x, c))))
        pl.when(mine & (z > 0) & (from_z >= z))(lambda: act(full_copy(slot, 1, index(z - 1, x, c))))
        pl.when((x < inner - 1) & (from_x <= x))(lambda: act(full_copy(slot, 2, index(z, x + 1, c))))
        pl.when((x > 0) & (from_x >= x))(lambda: act(full_copy(slot, 3, index(z, x - 1, c))))
        act(full_copy(slot, 4, index(z, x, 1 - c)))

    each_full(z, x, lambda copy: copy.start())

    real_high, real_low = split(a_ref[0])
    imag_high, imag_low = split(a_ref[1])
    stacked = jnp.concatenate([real_high, imag_high, real_low, imag_low], axis=0)
    chips = outer * inner

    def reorder(chip, carry):
        first, second = jnp.int32(0), jnp.int32(0)
        for b in range(n):
            first = first + jnp.where(owner_ref[b] == 2 * chip, b * rows, 0)
            second = second + jnp.where(owner_ref[b] == 2 * chip + 1, b * rows, 0)
        lane = lax.broadcasted_iota(jnp.int32, (total_rows, 2 * rows), 1)
        wanted = jnp.where(lane < rows, lane + first, lane - rows + second)
        chosen = lax.broadcasted_iota(jnp.int32, (total_rows, 2 * rows), 0) == wanted
        a4[chip] = dot(stacked, chosen.astype(F32).astype(BF16)).astype(BF16)
        return carry

    lax.fori_loop(0, chips, reorder, 0)

    off_all[index(0, x, c)] = jnp.zeros((2, rows, width), F32)

    own = index(0, x, c)

    def diagonal_step(t, carry):
        for i in range(inner):
            j = t - i

            @pl.when((j >= 0) & (j < outer))
            def _():
                from_z = nearest(z, j, outer)
                from_x = nearest(x, jnp.int32(i), inner)

                @pl.when((from_z != z) | (from_x != x))
                def _():
                    full_copy(index(from_z, from_x, c), 4, index(z, x, 1 - c)).wait_recv()
                    each_full(from_z, from_x, lambda copy: copy.start())

        for i in range(inner):
            j = t - 1 - i

            @pl.when((j >= 0) & (j < outer))
            def _():
                from_z = nearest(z, j, outer)
                from_x = nearest(x, jnp.int32(i), inner)
                full_copy(index(from_z, from_x, 1 - c), 4, index(z, x, 1 - c)).wait_recv()
                chip = from_z * inner + from_x
                slot = chip * 2
                right_real = jnp.concatenate([full[slot, 0], full[slot + 1, 0]], axis=0)
                right_imag = jnp.concatenate([full[slot, 1], full[slot + 1, 1]], axis=0)
                real, imag = pair_product(a4[chip], right_real, right_imag, rows)
                off_all[own, 0] = off_all[own, 0] + real
                off_all[own, 1] = off_all[own, 1] + imag

        return carry

    lax.fori_loop(0, outer + inner, diagonal_step, 0)

    off_real = -off_all[own, 0] * live
    off_imag = -off_all[own, 1] * live
    off_all[own, 0] = off_real
    off_all[own, 1] = off_imag

    def off_copy(slot, way, target):
        return pltpu.make_async_remote_copy(
            src_ref=off_all.at[slot], dst_ref=off_all.at[slot],
            send_sem=off_send.at[slot, way], recv_sem=off_recv.at[slot],
            device_id=(pole, target), device_id_type=pl.DeviceIdType.MESH,
        )

    def each_off(from_x, act):
        slot = index(0, from_x, c)
        pl.when((x < inner - 1) & (from_x <= x))(lambda: act(off_copy(slot, 0, index(z, x + 1, c))))
        pl.when((x > 0) & (from_x >= x))(lambda: act(off_copy(slot, 1, index(z, x - 1, c))))
        act(off_copy(slot, 2, index(z, x, 1 - c)))

    each_off(x, lambda copy: copy.start())

    weight_real, weight_imag = w_ref[0], w_ref[1]
    pole_off[pole, 0] = weight_real * off_real - weight_imag * off_imag
    pole_off[pole, 1] = weight_real * off_imag + weight_imag * off_real

    def pole_copy(buffer, send, recv, slot, other, way):
        return pltpu.make_async_remote_copy(
            src_ref=buffer.at[slot], dst_ref=buffer.at[slot],
            send_sem=send.at[way], recv_sem=recv.at[slot],
            device_id=(other, me), device_id_type=pl.DeviceIdType.MESH,
        )

    for k in range(1, poles):
        pole_copy(pole_off, po_send, po_recv, pole, (pole + k) % poles, k).start()

    for chip in range(inner):
        slot = index(z, chip, 0)
        at = slice(chip * 2 * rows, (chip + 1) * 2 * rows)
        for part in range(2):
            ft[part, :, at] = jnp.transpose(jnp.concatenate([full[slot, part], full[slot + 1, part]], axis=0))
    left = []
    for part in range(2):
        left.append(jnp.concatenate(
            [ft[part, pl.ds(pl.multiple_of(index(k, x, c) * share, share), share), :] for k in range(outer)], axis=0))
    left_rh, left_rl = split(left[0])
    left_ih, left_il = split(left[1])
    left4 = jnp.concatenate([left_rh, left_ih, left_rl, left_il], axis=0)

    for i in range(1, inner):
        from_x = nearest(x, jnp.int32(i), inner)
        off_copy(index(0, from_x, c), 2, index(z, x, 1 - c)).wait_recv()
        each_off(from_x, lambda copy: copy.start())
    for i in range(inner):
        off_copy(index(0, i, 1 - c), 2, index(z, x, 1 - c)).wait_recv()

    right_real = jnp.concatenate([off_all[k, 0] for k in range(group)], axis=0)
    right_imag = jnp.concatenate([off_all[k, 1] for k in range(group)], axis=0)
    gram_real, gram_imag = pair_product(left4, right_real, right_imag, outer * share)
    for k in range(outer):
        gram[k, 0] = gram_real[k * share : (k + 1) * share]
        gram[k, 1] = gram_imag[k * share : (k + 1) * share]

    def gram_copy(from_z, to_z, way):
        return pltpu.make_async_remote_copy(
            src_ref=gram.at[to_z], dst_ref=gram_in.at[from_z],
            send_sem=gram_send.at[way], recv_sem=gram_recv.at[from_z],
            device_id=(pole, index(to_z, x, c)), device_id_type=pl.DeviceIdType.MESH,
        )

    for k in range(1, outer):
        gram_copy(z, (z + k) % outer, k).start()
    real, imag = d_ref[0] - gram[z, 0], d_ref[1] - gram[z, 1]
    for k in range(1, outer):
        from_z = (z + k) % outer
        gram_copy(from_z, from_z, k).wait_recv()
        real, imag = real - gram_in[from_z, 0], imag - gram_in[from_z, 1]
    pole_diag[pole, 0] = weight_real * real - weight_imag * imag
    pole_diag[pole, 1] = weight_real * imag + weight_imag * real
    for k in range(1, poles):
        pole_copy(pole_diag, pd_send, pd_recv, pole, (pole + k) % poles, k).start()

    for k in range(1, poles):
        other = (pole + k) % poles
        pole_copy(pole_off, po_send, po_recv, other, other, k).wait_recv()
    total = pole_off[0]
    for k in range(1, poles):
        total = total + pole_off[k]
    off_out[...] = total

    def finish(slot, carry):
        each_full(slot // inner, slot % inner, lambda copy: copy.wait_send())
        return carry

    lax.fori_loop(0, chips, finish, 0)
    for i in range(inner):
        each_off(jnp.int32(i), lambda copy: copy.wait_send())
    for k in range(1, outer):
        gram_copy(z, (z + k) % outer, k).wait_send()
    for k in range(1, poles):
        pole_copy(pole_off, po_send, po_recv, pole, (pole + k) % poles, k).wait_send()
    for k in range(1, poles):
        other = (pole + k) % poles
        pole_copy(pole_diag, pd_send, pd_recv, other, other, k).wait_recv()
    total = pole_diag[0]
    for k in range(1, poles):
        total = total + pole_diag[k]
    diag_out[...] = total
    for k in range(1, poles):
        pole_copy(pole_diag, pd_send, pd_recv, pole, (pole + k) % poles, k).wait_send()


def per_device(dims, inverse_block, factor_block, diag_inverse, residues, block_owner, row_count):
    poles, outer, inner = dims
    _, _, rows, total_rows = inverse_block.shape
    width = factor_block.shape[3]
    share = diag_inverse.shape[2]
    n, group, chips = outer * inner * 2, inner * 2, outer * inner
    dma = pltpu.SemaphoreType.DMA
    vmem, smem = pl.BlockSpec(memory_space=pltpu.VMEM), pl.BlockSpec(memory_space=pltpu.SMEM)
    return pl.pallas_call(
        functools.partial(kernel, dims),
        out_shape=(
            jax.ShapeDtypeStruct((2, rows, width), F32),
            jax.ShapeDtypeStruct((2, share, width), F32),
        ),
        in_specs=[vmem, vmem, vmem, smem, smem, smem],
        out_specs=(vmem, vmem),
        scratch_shapes=[
            pltpu.VMEM((n, 2, rows, width), F32),
            pltpu.VMEM((chips, 4 * rows, 2 * rows), BF16),
            pltpu.VMEM((group, 2, rows, width), F32),
            pltpu.VMEM((2, width, group * rows), F32),
            pltpu.VMEM((outer, 2, share, width), F32),
            pltpu.VMEM((outer, 2, share, width), F32),
            pltpu.VMEM((poles, 2, rows, width), F32),
            pltpu.VMEM((poles, 2, share, width), F32),
            dma((n, 5)), dma((n,)), dma((group, 3)), dma((group,)), dma((outer,)), dma((outer,)),
            dma((poles,)), dma((poles,)), dma((poles,)), dma((poles,)),
        ],
        compiler_params=pltpu.CompilerParams(
            collective_id=0, has_side_effects=True, vmem_limit_bytes=56 * 1024 * 1024
        ),
    )(inverse_block[0], factor_block[0], diag_inverse[0], residues[0], block_owner, row_count)


def grid_lines(mesh):
    chips = mesh.shape["grid"] // 2
    inner = max(k for k in range(1, chips + 1) if chips % k == 0 and k * k <= chips)
    try:
        places = [tuple(device.coords) for device in mesh.devices.reshape(mesh.shape["poles"], -1)[0]][::2]
        moved = next(i for i in range(3) if places[1][i] != places[0][i])
        run = len({place[moved] for place in places})
        inner = run if chips % run == 0 else inner
    except (AttributeError, IndexError, StopIteration):
        pass
    return chips // inner, inner


def solution(mesh):
    placed = (
        P("poles", None, "grid", None),
        P("poles", None, "grid", None),
        P("poles", None, "grid", None),
        P("poles", None),
        P(),
        P(),
    )
    dims = (mesh.shape["poles"],) + grid_lines(mesh)
    return jax.shard_map(
        functools.partial(per_device, dims),
        mesh=mesh,
        in_specs=placed,
        out_specs=(P(None, "grid", None), P(None, "grid", None)),
        check_vma=False,
    )
```

time: 179 us -> 63.2 us (0.35)
  waiting for transfers between devices: 114 us -> 0 us
  Pallas kernels: 0 us -> 59.5 us
  other arithmetic: 26.3 us -> 0 us
  between operations: 13.9 us -> 0.65 us
  matrix products: 12.6 us -> 0 us
  local copies, waits for them, and re-layouts: 11.6 us -> 2.37 us
    pallas_call x0 -> x1, Pallas kernels: none -> 59.5 us  [per_device(): pl.pallas_call(functools.partial(kernel, dims), out_shape=(jax.ShapeDtype...]
    reduce_scatter x1 -> x0, waiting for transfers between devices: 56.8 us -> none  [per_device(): row_share = lax.psum_scatter(gram, 'grid', scatter_dimension=1, tiled=True)]
    all_gather x1 -> x0, waiting for transfers between devices: 32.3 us -> none  [per_device(): shard_piece = lax.all_gather(masked, 'grid', axis=1, tiled=True)]
    psum x1 -> x0, waiting for transfers between devices: 25.1 us -> none  [per_device(): lax.psum((weigh(weights, offdiag), diag_term), 'poles')]
    dot_general x8 -> x0, matrix products: 12.6 us -> none  [product(): jnp.dot(left, right, preferred_element_type=jnp.float32, precision=HIGHES...]
    and x1 -> x0, other arithmetic: 5.65 us -> none  [per_device(): jnp.take(inverse_rows, natural_columns(inverse_of, shard_piece.shape[1],...]
    gather x11 -> x0, other arithmetic: 4.66 us -> none  [the longest x10 4.65 us: natural_columns(): return inverse_of[stored // own_rows] * own_rows + stored % own_rows]
    gather x2 -> x0, local copies, waits for them, and re-layouts: 4.25 us -> none  [the longest x1 3.54 us: per_device(): jnp.take(inverse_rows, natural_columns(inverse_of, shard_piece.shape[1],...]
  transfers between devices with their start and end apart: 3 -> 0, of which waited for: 3 -> 0; matrix products, arithmetic and copies ran while one was open for 13% -> 0% of each run, Pallas kernels for 0% -> 0%
where the time goes in v1:
time: 63.2 us; the launch traced here: 62.5 us
  Pallas kernels  59.5 us (94%)
  local copies, waits for them, and re-layouts  2.37 us (4%)
  between operations  0.65 us (1%)
    pallas_call x1, Pallas kernels, per_device(): pl.pallas_call(functools.partial(kernel, dims), out_shape=(jax.ShapeDtype...  59.5 us
    unnamed x4, local copies, waits for them, and re-layouts  2.37 us

profile of v1, /device:TPU:0, one launch (start us, length us, event | category | flops | bytes accessed | tf_op | source)
XLA Modules:
  0.0 62.5 jit_solution(9377919735839446481)
XLA Ops:
  0.6 59.5 %shard_map.77 = (f32[2,64,512]{2,1,0:T(8,128)}, f32[2,32,512]{2,1,0:T(8,128)}) custom-call(f32[2,64,1024]{2,1,0:T(8,128)} %bitcast.4, f32[2,64,512]{2,1,0:T(8,128)} %bitcast.5, f32[2,32,512]{2,1,0:T(8,128)} %bitcast.6, f32[2]{0:T(128)} %bitcast.7, s32[16]{0:T(128)} %owner_ref.1, s32[16]{0:T(128)} %count_ref.1), custom_call_target="tpu_custom_call" | custom-call | tf_op jit(solution)/shard_map/pallas_call | solution.py:276
  60.1 0.0 copy-start
  60.1 1.7 %copy.10 = f32[2,64,512]{2,1,0:T(8,128)} copy(f32[2,64,512]{2,1,0:T(8,128)} %get-tuple-element.4) | data formatting | bytes 524288
  61.8 0.0 copy-done
  61.8 0.7 %copy.11 = f32[2,32,512]{2,1,0:T(8,128)} copy(f32[2,32,512]{2,1,0:T(8,128)S(1)} %copy-done) | data formatting | bytes 262144
Async XLA Ops:
  60.1 1.7 %copy-start = (f32[2,32,512]{2,1,0:T(8,128)S(1)}, f32[2,32,512]{2,1,0:T(8,128)}, u32[]{:S(2)}) copy-start(f32[2,32,512]{2,1,0:T(8,128)} %get-tuple-element.5) | copy-start | bytes 393220

commit v2 on v1

v2 whole, which is shorter than its diff:
```python
import functools

import jax
import jax.numpy as jnp
from jax import lax
from jax.experimental import pallas as pl
from jax.experimental.pallas import tpu as pltpu
from jax.sharding import PartitionSpec as P

BF16 = jnp.bfloat16
F32 = jnp.float32
SKEW = 2
CHUNKS = 2


def split(values):
    high = values.astype(BF16)
    return high, (values - high.astype(F32)).astype(BF16)


def dot(left, right):
    return jnp.dot(left, right, preferred_element_type=F32)


def pair_product(left4, right_real, right_imag, rows):
    width = right_real.shape[1]
    real_high, real_low = split(right_real)
    imag_high, imag_low = split(right_imag)
    first = dot(left4, jnp.concatenate([real_high, imag_high], axis=1))
    second = dot(left4[: 2 * rows], jnp.concatenate([real_low, imag_low], axis=1))
    by_real = first[: 2 * rows] + first[2 * rows :] + second
    rr, ri = by_real[:rows, :width], by_real[:rows, width:]
    ir, ii = by_real[rows:, :width], by_real[rows:, width:]
    return rr - ii, ri + ir


def nearest(place, step, amount):
    near = jnp.minimum(place, amount - 1 - place)
    half = (step + 1) // 2
    both = jnp.where(step % 2 == 1, place + half, place - half)
    far = jnp.where(place < amount - 1 - place, place + (step - near), place - (step - near))
    return jnp.where(step <= 2 * near, both, far)


def kernel(
    dims, a_ref, f_ref, d_ref, w_ref, owner_ref, count_ref, off_out, diag_out,
    full, a4, off_all, ft, left4, gram, gram_in, pole_off, pole_diag,
    full_send, full_recv, off_send, off_recv, gram_send, gram_recv, po_send, po_recv, pd_send, pd_recv,
):
    poles, outer, inner = dims
    n = outer * inner * 2
    group = inner * 2
    rows, width = f_ref.shape[1], f_ref.shape[2]
    total_rows = a_ref.shape[2]
    share = d_ref.shape[1]
    chunks = full.shape[0]
    wide = width // chunks
    me = lax.axis_index("grid")
    pole = lax.axis_index("poles")
    z, x, c = me // group, (me // 2) % inner, me % 2

    def index(at_z, at_x, at_c):
        return at_z * group + at_x * 2 + at_c

    barrier = pltpu.get_barrier_semaphore()

    def greet(target):
        pl.semaphore_signal(barrier, inc=1, device_id=target, device_id_type=pl.DeviceIdType.MESH)

    greet((pole, index(z, x, 1 - c)))
    for k in range(1, outer):
        greet((pole, index((z + k) % outer, x, c)))
    for k in range(1, poles):
        greet(((pole + k) % poles, me))
    pl.when(x > 0)(lambda: greet((pole, index(z, x - 1, c))))
    pl.when(x < inner - 1)(lambda: greet((pole, index(z, x + 1, c))))

    live_count = jnp.int32(0)
    for b in range(n):
        live_count = live_count + jnp.where(owner_ref[b] == me, count_ref[b], 0)
    live = (lax.broadcasted_iota(jnp.int32, (rows, width), 0) < live_count).astype(F32)
    for h in range(chunks):
        for part in range(2):
            full[h, me, part] = f_ref[part, :, h * wide : (h + 1) * wide] * live[:, :wide]

    beside = jnp.where(x > 0, 1, 0) + jnp.where(x < inner - 1, 1, 0)
    pl.semaphore_wait(barrier, outer + poles - 1 + beside)

    def full_copy(h, slot, way, target):
        return pltpu.make_async_remote_copy(
            src_ref=full.at[h, slot], dst_ref=full.at[h, slot],
            send_sem=full_send.at[h, slot, way], recv_sem=full_recv.at[h, slot],
            device_id=(pole, target), device_id_type=pl.DeviceIdType.MESH,
        )

    def each_full(h, from_z, from_x, act):
        slot = index(from_z, from_x, c)
        mine = from_x == x
        pl.when(mine & (z < outer - 1) & (from_z <= z))(lambda: act(full_copy(h, slot, 0, index(z + 1, x, c))))
        pl.when(mine & (z > 0) & (from_z >= z))(lambda: act(full_copy(h, slot, 1, index(z - 1, x, c))))
        pl.when((x < inner - 1) & (from_x <= x))(lambda: act(full_copy(h, slot, 2, index(z, x + 1, c))))
        pl.when((x > 0) & (from_x >= x))(lambda: act(full_copy(h, slot, 3, index(z, x - 1, c))))
        act(full_copy(h, slot, 4, index(z, x, 1 - c)))

    def start(copy):
        copy.start()

    for h in range(chunks):
        each_full(h, z, x, start)

    real_high, real_low = split(a_ref[0])
    imag_high, imag_low = split(a_ref[1])
    stacked = jnp.concatenate([real_high, imag_high, real_low, imag_low], axis=0)
    chips = outer * inner

    def reorder(chip, carry):
        first, second = jnp.int32(0), jnp.int32(0)
        for b in range(n):
            first = first + jnp.where(owner_ref[b] == 2 * chip, b * rows, 0)
            second = second + jnp.where(owner_ref[b] == 2 * chip + 1, b * rows, 0)
        lane = lax.broadcasted_iota(jnp.int32, (total_rows, 2 * rows), 1)
        wanted = jnp.where(lane < rows, lane + first, lane - rows + second)
        chosen = lax.broadcasted_iota(jnp.int32, (total_rows, 2 * rows), 0) == wanted
        a4[chip] = dot(stacked, chosen.astype(F32).astype(BF16)).astype(BF16)
        return carry

    lax.fori_loop(0, chips, reorder, 0)

    own = index(0, x, c)

    def make_rows():
        for h in range(chunks):
            for chip in range(inner):
                slot = index(z, chip, 0)
                at = slice(chip * 2 * rows, (chip + 1) * 2 * rows)
                for part in range(2):
                    ft[part, h * wide : (h + 1) * wide, at] = jnp.transpose(
                        jnp.concatenate([full[h, slot, part], full[h, slot + 1, part]], axis=0))
        left = []
        for part in range(2):
            left.append(jnp.concatenate(
                [ft[part, pl.ds(pl.multiple_of(index(k, x, c) * share, share), share), :] for k in range(outer)],
                axis=0))
        left_rh, left_rl = split(left[0])
        left_ih, left_il = split(left[1])
        left4[...] = jnp.concatenate([left_rh, left_ih, left_rl, left_il], axis=0)

    weight_real, weight_imag = w_ref[0], w_ref[1]

    def off_copy(h, slot, way, target):
        return pltpu.make_async_remote_copy(
            src_ref=off_all.at[h, slot], dst_ref=off_all.at[h, slot],
            send_sem=off_send.at[h, slot, way], recv_sem=off_recv.at[h, slot],
            device_id=(pole, target), device_id_type=pl.DeviceIdType.MESH,
        )

    def each_off(h, from_x, act):
        slot = index(0, from_x, c)
        pl.when((x < inner - 1) & (from_x <= x))(lambda: act(off_copy(h, slot, 0, index(z, x + 1, c))))
        pl.when((x > 0) & (from_x >= x))(lambda: act(off_copy(h, slot, 1, index(z, x - 1, c))))
        act(off_copy(h, slot, 2, index(z, x, 1 - c)))

    def pole_copy(h, buffer, send, recv, slot, other, way):
        return pltpu.make_async_remote_copy(
            src_ref=buffer.at[h, slot], dst_ref=buffer.at[h, slot],
            send_sem=send.at[h, way], recv_sem=recv.at[h, slot],
            device_id=(other, me), device_id_type=pl.DeviceIdType.MESH,
        )

    def gram_copy(h, from_z, to_z, way):
        return pltpu.make_async_remote_copy(
            src_ref=gram.at[h, to_z], dst_ref=gram_in.at[h, from_z],
            send_sem=gram_send.at[h, way], recv_sem=gram_recv.at[h, from_z],
            device_id=(pole, index(to_z, x, c)), device_id_type=pl.DeviceIdType.MESH,
        )

    last = outer + inner - 1
    for h in range(chunks):
        off_all[h, own] = jnp.zeros((2, rows, wide), F32)

    def relay(h, t):
        for i in range(inner):
            j = t - i

            @pl.when((j >= 0) & (j < outer) & (t > 0))
            def _():
                from_z = nearest(z, j, outer)
                from_x = nearest(x, jnp.int32(i), inner)
                full_copy(h, index(from_z, from_x, c), 4, index(z, x, 1 - c)).wait_recv()
                each_full(h, from_z, from_x, start)

    def multiply(h, t):
        for i in range(inner):
            j = t - 1 - i

            @pl.when((j >= 0) & (j < outer))
            def _():
                from_z = nearest(z, j, outer)
                from_x = nearest(x, jnp.int32(i), inner)
                full_copy(h, index(from_z, from_x, 1 - c), 4, index(z, x, 1 - c)).wait_recv()
                chip = from_z * inner + from_x
                slot = chip * 2
                right_real = jnp.concatenate([full[h, slot, 0], full[h, slot + 1, 0]], axis=0)
                right_imag = jnp.concatenate([full[h, slot, 1], full[h, slot + 1, 1]], axis=0)
                real, imag = pair_product(a4[chip], right_real, right_imag, rows)
                off_all[h, own, 0] = off_all[h, own, 0] + real
                off_all[h, own, 1] = off_all[h, own, 1] + imag

    def gather(first):
        def step(t, carry):
            for h in range(first, chunks):
                relay(h, t - SKEW * h)
            for h in range(first, chunks):
                multiply(h, t - SKEW * h)
            return carry

        begin = 1 if first == 0 else last + 1 + SKEW * (first - 1)
        lax.fori_loop(begin, last + 1 + SKEW * first, step, 0)

    def finish_rows(h):
        off_real = -off_all[h, own, 0] * live[:, :wide]
        off_imag = -off_all[h, own, 1] * live[:, :wide]
        off_all[h, own, 0] = off_real
        off_all[h, own, 1] = off_imag
        each_off(h, x, start)
        pole_off[h, pole, 0] = weight_real * off_real - weight_imag * off_imag
        pole_off[h, pole, 1] = weight_real * off_imag + weight_imag * off_real
        for k in range(1, poles):
            pole_copy(h, pole_off, po_send, po_recv, pole, (pole + k) % poles, k).start()

    def make_gram(h):
        for i in range(1, inner):
            from_x = nearest(x, jnp.int32(i), inner)
            off_copy(h, index(0, from_x, c), 2, index(z, x, 1 - c)).wait_recv()
            each_off(h, from_x, start)
        for i in range(inner):
            off_copy(h, index(0, i, 1 - c), 2, index(z, x, 1 - c)).wait_recv()
        right_real = jnp.concatenate([off_all[h, k, 0] for k in range(group)], axis=0)
        right_imag = jnp.concatenate([off_all[h, k, 1] for k in range(group)], axis=0)
        gram_real, gram_imag = pair_product(left4[...], right_real, right_imag, outer * share)
        for k in range(outer):
            gram[h, k, 0] = gram_real[k * share : (k + 1) * share]
            gram[h, k, 1] = gram_imag[k * share : (k + 1) * share]
        for k in range(1, outer):
            gram_copy(h, z, (z + k) % outer, k).start()

    def sum_gram(h):
        at = slice(h * wide, (h + 1) * wide)
        real, imag = d_ref[0, :, at] - gram[h, z, 0], d_ref[1, :, at] - gram[h, z, 1]
        for k in range(1, outer):
            from_z = (z + k) % outer
            gram_copy(h, from_z, from_z, k).wait_recv()
            real, imag = real - gram_in[h, from_z, 0], imag - gram_in[h, from_z, 1]
        pole_diag[h, pole, 0] = weight_real * real - weight_imag * imag
        pole_diag[h, pole, 1] = weight_real * imag + weight_imag * real
        for k in range(1, poles):
            pole_copy(h, pole_diag, pd_send, pd_recv, pole, (pole + k) % poles, k).start()

    for h in range(chunks + 2):
        if h < chunks:
            gather(h)
            finish_rows(h)
        if h == 1:
            make_rows()
        if 1 <= h <= chunks:
            make_gram(h - 1)
        if h >= 2:
            sum_gram(h - 2)

    def add_poles(h, buffer, send, recv, out):
        for k in range(1, poles):
            other = (pole + k) % poles
            pole_copy(h, buffer, send, recv, other, other, k).wait_recv()
        total = buffer[h, 0]
        for k in range(1, poles):
            total = total + buffer[h, k]
        out[:, :, h * wide : (h + 1) * wide] = total

    for h in range(chunks):
        add_poles(h, pole_off, po_send, po_recv, off_out)

    def finish(slot, carry):
        for h in range(chunks):
            each_full(h, slot // inner, slot % inner, lambda copy: copy.wait_send())
        return carry

    lax.fori_loop(0, chips, finish, 0)
    for h in range(chunks):
        for i in range(inner):
            each_off(h, jnp.int32(i), lambda copy: copy.wait_send())
        for k in range(1, outer):
            gram_copy(h, z, (z + k) % outer, k).wait_send()
        for k in range(1, poles):
            pole_copy(h, pole_off, po_send, po_recv, pole, (pole + k) % poles, k).wait_send()
    for h in range(chunks):
        add_poles(h, pole_diag, pd_send, pd_recv, diag_out)
        for k in range(1, poles):
            pole_copy(h, pole_diag, pd_send, pd_recv, pole, (pole + k) % poles, k).wait_send()


def per_device(dims, inverse_block, factor_block, diag_inverse, residues, block_owner, row_count):
    poles, outer, inner = dims
    _, _, rows, total_rows = inverse_block.shape
    width = factor_block.shape[3]
    share = diag_inverse.shape[2]
    n, group, chips = outer * inner * 2, inner * 2, outer * inner
    dma = pltpu.SemaphoreType.DMA
    chunks = CHUNKS if width % (128 * CHUNKS) == 0 else 1
    wide = width // chunks
    vmem, smem = pl.BlockSpec(memory_space=pltpu.VMEM), pl.BlockSpec(memory_space=pltpu.SMEM)
    return pl.pallas_call(
        functools.partial(kernel, dims),
        out_shape=(
            jax.ShapeDtypeStruct((2, rows, width), F32),
            jax.ShapeDtypeStruct((2, share, width), F32),
        ),
        in_specs=[vmem, vmem, vmem, smem, smem, smem],
        out_specs=(vmem, vmem),
        scratch_shapes=[
            pltpu.VMEM((chunks, n, 2, rows, wide), F32),
            pltpu.VMEM((chips, 4 * rows, 2 * rows), BF16),
            pltpu.VMEM((chunks, group, 2, rows, wide), F32),
            pltpu.VMEM((2, width, group * rows), F32),
            pltpu.VMEM((4 * outer * share, group * rows), BF16),
            pltpu.VMEM((chunks, outer, 2, share, wide), F32),
            pltpu.VMEM((chunks, outer, 2, share, wide), F32),
            pltpu.VMEM((chunks, poles, 2, rows, wide), F32),
            pltpu.VMEM((chunks, poles, 2, share, wide), F32),
            dma((chunks, n, 5)), dma((chunks, n)), dma((chunks, group, 3)), dma((chunks, group)),
            dma((chunks, outer)), dma((chunks, outer)),
            dma((chunks, poles)), dma((chunks, poles)), dma((chunks, poles)), dma((chunks, poles)),
        ],
        compiler_params=pltpu.CompilerParams(
            collective_id=0, has_side_effects=True, vmem_limit_bytes=56 * 1024 * 1024
        ),
    )(inverse_block[0], factor_block[0], diag_inverse[0], residues[0], block_owner, row_count)


def grid_lines(mesh):
    chips = mesh.shape["grid"] // 2
    inner = max(k for k in range(1, chips + 1) if chips % k == 0 and k * k <= chips)
    try:
        places = [tuple(device.coords) for device in mesh.devices.reshape(mesh.shape["poles"], -1)[0]][::2]
        moved = next(i for i in range(3) if places[1][i] != places[0][i])
        run = len({place[moved] for place in places})
        inner = run if chips % run == 0 else inner
    except (AttributeError, IndexError, StopIteration):
        pass
    return chips // inner, inner


def solution(mesh):
    placed = (
        P("poles", None, "grid", None),
        P("poles", None, "grid", None),
        P("poles", None, "grid", None),
        P("poles", None),
        P(),
        P(),
    )
    dims = (mesh.shape["poles"],) + grid_lines(mesh)
    return jax.shard_map(
        functools.partial(per_device, dims),
        mesh=mesh,
        in_specs=placed,
        out_specs=(P(None, "grid", None), P(None, "grid", None)),
        check_vma=False,
    )
```

time: 63.2 us -> 58.1 us (0.919)
  Pallas kernels: 59.5 us -> 54.9 us
    pallas_call x1, Pallas kernels: 59.5 us -> 54.9 us  [per_device(): pl.pallas_call(functools.partial(kernel, dims), out_shape=(jax.ShapeDtype...]
where the time goes in v2:
time: 58.1 us; the launch traced here: 57.9 us
  Pallas kernels  54.9 us (94%)
  local copies, waits for them, and re-layouts  2.37 us (4%)
  between operations  0.65 us (1%)
    pallas_call x1, Pallas kernels, per_device(): pl.pallas_call(functools.partial(kernel, dims), out_shape=(jax.ShapeDtype...  54.9 us
    unnamed x4, local copies, waits for them, and re-layouts  2.37 us

profile of v2, /device:TPU:0, one launch (start us, length us, event | category | flops | bytes accessed | tf_op | source)
XLA Modules:
  0.0 57.9 jit_solution(14521295590888316847)
XLA Ops:
  0.6 54.9 %shard_map.77 = (f32[2,64,512]{2,1,0:T(8,128)}, f32[2,32,512]{2,1,0:T(8,128)}) custom-call(f32[2,64,1024]{2,1,0:T(8,128)} %bitcast.4, f32[2,64,512]{2,1,0:T(8,128)} %bitcast.5, f32[2,32,512]{2,1,0:T(8,128)} %bitcast.6, f32[2]{0:T(128)} %bitcast.7, s32[16]{0:T(128)} %owner_ref.1, s32[16]{0:T(128)} %count_ref.1), custom_call_target="tpu_custom_call" | custom-call | tf_op jit(solution)/shard_map/pallas_call | solution.py:311
  55.5 0.0 copy-start
  55.5 1.7 %copy.10 = f32[2,64,512]{2,1,0:T(8,128)} copy(f32[2,64,512]{2,1,0:T(8,128)} %get-tuple-element.4) | data formatting | bytes 524288
  57.2 0.0 copy-done
  57.2 0.7 %copy.11 = f32[2,32,512]{2,1,0:T(8,128)} copy(f32[2,32,512]{2,1,0:T(8,128)S(1)} %copy-done) | data formatting | bytes 262144
Async XLA Ops:
  55.5 1.7 %copy-start = (f32[2,32,512]{2,1,0:T(8,128)S(1)}, f32[2,32,512]{2,1,0:T(8,128)}, u32[]{:S(2)}) copy-start(f32[2,32,512]{2,1,0:T(8,128)} %get-tuple-element.5) | copy-start | bytes 393220

commit v3 on v2

--- a/solution.py
+++ b/solution.py
@@ -10,6 +10,7 @@
 BF16 = jnp.bfloat16
 F32 = jnp.float32
 SKEW = 2
+LAG = 2
 CHUNKS = 2
 
 
@@ -174,13 +175,13 @@
             device_id=(pole, index(to_z, x, c)), device_id_type=pl.DeviceIdType.MESH,
         )
 
-    last = outer + inner - 1
+    last = outer + LAG * (inner - 1)
     for h in range(chunks):
         off_all[h, own] = jnp.zeros((2, rows, wide), F32)
 
     def relay(h, t):
         for i in range(inner):
-            j = t - i
+            j = t - LAG * i
 
             @pl.when((j >= 0) & (j < outer) & (t > 0))
             def _():
@@ -191,7 +192,7 @@
 
     def multiply(h, t):
         for i in range(inner):
-            j = t - 1 - i
+            j = t - 1 - LAG * i
 
             @pl.when((j >= 0) & (j < outer))
             def _():

time: 58.1 us -> 57.2 us (0.985)
  Pallas kernels: 54.9 us -> 54 us
    pallas_call x1, Pallas kernels: 54.9 us -> 54 us  [per_device(): pl.pallas_call(functools.partial(kernel, dims), out_shape=(jax.ShapeDtype...]
where the time goes in v3:
time: 57.2 us; the launch traced here: 57.1 us
  Pallas kernels  54 us (94%)
  local copies, waits for them, and re-layouts  2.37 us (4%)
  between operations  0.65 us (1%)
    pallas_call x1, Pallas kernels, per_device(): pl.pallas_call(functools.partial(kernel, dims), out_shape=(jax.ShapeDtype...  54 us
    unnamed x4, local copies, waits for them, and re-layouts  2.37 us

profile of v3, /device:TPU:0, one launch (start us, length us, event | category | flops | bytes accessed | tf_op | source)
XLA Modules:
  0.0 57.1 jit_solution(11498390260173333760)
XLA Ops:
  0.6 54.0 %shard_map.77 = (f32[2,64,512]{2,1,0:T(8,128)}, f32[2,32,512]{2,1,0:T(8,128)}) custom-call(f32[2,64,1024]{2,1,0:T(8,128)} %bitcast.4, f32[2,64,512]{2,1,0:T(8,128)} %bitcast.5, f32[2,32,512]{2,1,0:T(8,128)} %bitcast.6, f32[2]{0:T(128)} %bitcast.7, s32[16]{0:T(128)} %owner_ref.1, s32[16]{0:T(128)} %count_ref.1), custom_call_target="tpu_custom_call" | custom-call | tf_op jit(solution)/shard_map/pallas_call | solution.py:312
  54.7 0.0 copy-start
  54.7 1.7 %copy.10 = f32[2,64,512]{2,1,0:T(8,128)} copy(f32[2,64,512]{2,1,0:T(8,128)} %get-tuple-element.4) | data formatting | bytes 524288
  56.4 0.0 copy-done
  56.4 0.7 %copy.11 = f32[2,32,512]{2,1,0:T(8,128)} copy(f32[2,32,512]{2,1,0:T(8,128)S(1)} %copy-done) | data formatting | bytes 262144
Async XLA Ops:
  54.7 1.7 %copy-start = (f32[2,32,512]{2,1,0:T(8,128)S(1)}, f32[2,32,512]{2,1,0:T(8,128)}, u32[]{:S(2)}) copy-start(f32[2,32,512]{2,1,0:T(8,128)} %get-tuple-element.5) | copy-start | bytes 393220
